TPU v7x, 32 devices: a whole 2x2x4 slice. The times are simulated.
32 devices in a mesh: section: 4 (over y, core), phase: 2 (over x), tp: 4 (over z).
Axes of the slice: x: 2, y: 2, z: 4, core: 2. Of those that a mesh axis runs over, the one named last changes fastest.
Arguments:
- hidden_act: bfloat16 [1024, 28672], P(('section', 'phase'), 'tp'), may hold values from -6 to 6
- down_weight: bfloat16 [28672, 8192], P('tp', ('phase', 'section')), may hold values from -0.03125 to 0.03125
- residual: bfloat16 [1024, 8192], P('section', 'phase'), may hold values from -6 to 6
- head_weight: float32 [8192], P('phase'), may hold values from -0.011048543 to 0.011048543
- gain: float32 [8192], P('phase'), may hold values from 0.1 to 1.9
- behavior_policy_logprob: float32 [1024], replicated, may hold values from -6 to -0.05
- frozen_policy_logprob: float32 [1024], replicated, may hold values from -6 to -0.05
- old_values: float32 [1024], replicated, may hold values from -5 to 5
- judge_ratings: float32 [16], replicated, may hold values from -8 to 8
- lengths: int32 [16], replicated, may hold values from 1 to 192, 1024 in all
Outputs:
- total_loss: float32 [], replicated
- head_grad: float32 [8192], P('phase')
- down_projection_gradient: float32 [28672, 8192], P('tp', ('phase', 'section'))
- hidden_grad: bfloat16 [1024, 28672], P(('section', 'phase'), 'tp')
Inputs may be any that keep to these rules, and one draw needn't show every extreme that they name: The 16 lengths sum to 1024; the longest is exactly 192.
All inputs are finite; a program needn't handle non-finite values.
Results may differ from a plain program's by a relative error of at most 0.0049.
Values may be sent and summed in bfloat16 or wider, within the bound.
A program may use at most 192 MiB of HBM per device.

v0:
```python
import functools

import jax
import jax.numpy as jnp
from jax import lax
from jax.experimental import pallas as pl
from jax.experimental.layout import Layout, with_layout_constraint
from jax.experimental.pallas import tpu as pltpu
from jax.sharding import PartitionSpec as P

D = 8192

KL_PENALTY_SCALE = 0.1
TRACE_DECAY = 0.95
CLIP_RANGE = 0.2
EPSILON = 1e-05
BF16 = jnp.bfloat16
F32 = jnp.float32


def returns_at(row_pos, behavior, frozen, old_values, judge_ratings, lengths):
    total = behavior.shape[0]
    position = jnp.arange(total, dtype=jnp.int32)
    ends = jnp.cumsum(lengths)
    closes = position[:, None] == ends[None, :] - 1
    final = jnp.any(closes, axis=1)
    extra = jnp.sum(jnp.where(closes, judge_ratings[None, :], 0.0), axis=1)
    payoff = extra - KL_PENALTY_SCALE * (behavior - frozen)
    following = jnp.concatenate([old_values[1:], jnp.zeros_like(old_values[:1])])
    following = jnp.where(final, 0.0, following)
    delta = payoff + following - old_values
    segment = jnp.sum((position[:, None] >= ends[None, :]).astype(jnp.int32), axis=1)
    row_seg = jnp.sum((row_pos[:, None] >= ends[None, :]).astype(jnp.int32), axis=1)
    gap = position[None, :] - row_pos[:, None]
    inside = (row_seg[:, None] == segment[None, :]) & (gap >= 0)
    powers = jnp.power(F32(TRACE_DECAY), jnp.maximum(gap, 0).astype(F32))
    advantage = jnp.sum(jnp.where(inside, powers, 0.0) * delta[None, :], axis=1)
    own_old = jnp.sum(jnp.where(gap == 0, old_values[None, :], 0.0), axis=1)
    return advantage + own_old, own_old


def exchange_kernel(axes, sizes, x_ref, out_ref, slots, send_sems, recv_sems):
    n0, n1 = sizes
    n = n0 * n1
    a, b = lax.axis_index(axes[0]), lax.axis_index(axes[1])
    me = a * n1 + b

    def partner(i):
        return {axes[0]: lax.rem(a + i // n1, n0), axes[1]: lax.rem(b + i % n1, n1)}

    barrier = pltpu.get_barrier_semaphore()
    for i in range(1, n):
        pl.semaphore_signal(barrier, inc=1, device_id=partner(i), device_id_type=pl.DeviceIdType.MESH)
    pl.semaphore_wait(barrier, n - 1)
    copies = []
    for i in range(1, n):
        copy = pltpu.make_async_remote_copy(
            src_ref=x_ref, dst_ref=slots.at[me], send_sem=send_sems.at[i], recv_sem=recv_sems.at[i],
            device_id=partner(i), device_id_type=pl.DeviceIdType.MESH,
        )
        copy.start()
        copies.append(copy)
    slots[me] = x_ref[...]
    for copy in copies:
        copy.wait()
    out_ref[...] = slots[...]


def share(x, axes, sizes, collective_id):
    count = x.size
    tiles = -(-count // 1024) * 8
    flat = jnp.pad(x.reshape(-1), (0, tiles * 128 - count)).reshape(tiles, 128)
    n = sizes[0] * sizes[1]
    out = pl.pallas_call(
        functools.partial(exchange_kernel, axes, sizes),
        out_shape=jax.ShapeDtypeStruct((n, tiles, 128), F32),
        in_specs=[pl.BlockSpec(memory_space=pltpu.VMEM)],
        out_specs=pl.BlockSpec(memory_space=pltpu.VMEM),
        scratch_shapes=[
            pltpu.VMEM((n, tiles, 128), F32),
            pltpu.SemaphoreType.DMA((n,)),
            pltpu.SemaphoreType.DMA((n,)),
        ],
        compiler_params=pltpu.CompilerParams(collective_id=collective_id, has_side_effects=True),
    )(flat)
    return out.reshape(n, -1)[:, :count].reshape((n,) + x.shape)


def on_device(mesh_shape, hidden_act, down_weight, residual, head_weight, gain,
              behavior, frozen, old_values, judge_ratings, lengths):
    S, Q, T = mesh_shape["section"], mesh_shape["phase"], mesh_shape["tp"]
    s, p, t = (lax.axis_index(a) for a in ("section", "phase", "tp"))
    rows, FF = hidden_act.shape
    C = down_weight.shape[1]
    K = 2 if rows % (4 * T) == 0 else 1
    piece = rows // (2 * K)
    sub = piece // T
    sizes = {"section": S, "phase": Q, "tp": T}

    def xchg(x, axis, mask):
        return lax.ppermute(x, axis, [(i, i ^ mask) for i in range(sizes[axis])])

    phase_steps = [("phase", 1 << i) for i in range(Q.bit_length() - 1)]
    section_steps = [("section", 1 << i) for i in range(1, S.bit_length() - 1)]
    orders = [phase_steps + section_steps, section_steps + phase_steps]
    held = []
    for steps in orders:
        rs = [0]
        for axis, mask in steps:
            bit = mask * Q if axis == "section" else mask
            rs = rs + [r ^ bit for r in rs]
        held.append(rs)
    nb = len(held[0])
    me = s * Q + p
    own = hidden_act.reshape(K, 2, 1, piece, FF)

    def after(x, *others):
        for y in others:
            x = x + (0 * y[(0,) * y.ndim]).astype(x.dtype)
        return x

    def residual_parts(token):
        res = after(residual, token).reshape(Q, K, 2, T, sub, S, C)
        res = lax.dynamic_index_in_dim(res, t, 3, keepdims=False)
        for i in range(Q.bit_length() - 1):
            pairs = res.reshape((Q >> (i + 1), 2, 1 << i) + res.shape[1:])
            pairs = jnp.where((p >> i) & 1 == 1, pairs[:, ::-1], pairs)
            res = pairs.reshape(res.shape)
        res_by = []
        for m in range(S):
            part = lax.dynamic_index_in_dim(res, s ^ m, 4, keepdims=False)
            res_by.append(part if m == 0 else xchg(part, "section", m))
        return res_by

    def reduce_tp(x):
        n, bit = T, 1
        while n > 1:
            y = x.reshape(x.shape[0], n // 2, 2, sub, C)
            up = (t & bit) != 0
            send = jnp.where(up, y[:, :, 0], y[:, :, 1]).astype(BF16)
            keep = jnp.where(up, y[:, :, 1], y[:, :, 0])
            x = keep + xchg(send, "tp", bit).astype(F32)
            n, bit = n // 2, bit * 2
        return x.reshape(-1, sub, C)

    def gather_tp(x):
        x = x[:, None]
        bit = T // 2
        while bit >= 1:
            got = xchg(x, "tp", bit)
            up = (t & bit) != 0
            lo, hi = jnp.where(up, got, x), jnp.where(up, x, got)
            x = jnp.stack([lo, hi], axis=2).reshape(x.shape[0], -1, sub, C)
            bit //= 2
        return x

    scale = lax.dynamic_slice_in_dim(gain * head_weight, s * C, C, 0)
    turned = with_layout_constraint(down_weight.T, Layout((0, 1)))
    pieces = [None] * K
    combined = [None] * K
    first, second, third = [], [], []
    for k in range(K):
        cur = [after(own[k, h], *first) for h in range(2)]
        for j in range(len(orders[0])):
            got = [xchg(cur[h], *orders[h][j]) for h in range(2)]
            cur = [jnp.concatenate([cur[h], got[h]], axis=0) for h in range(2)]
            if j == 0:
                cur = [after(x, *second) for x in cur]
        here = after(jnp.stack(cur), *third)
        pieces[k] = [here, xchg(here, "section", 1)]
        if k == 0:
            res_by = residual_parts(got[0])
        outs = [
            jnp.dot(pieces[k][c].reshape(-1, FF), down_weight, preferred_element_type=F32)
            .reshape(2 * nb, T, sub, C)
            for c in range(2)
        ]
        base = []
        for c in range(2):
            for h in range(2):
                for r in held[h]:
                    rr = r ^ (c * Q)
                    base.append(res_by[rr // Q][rr % Q, k, h])
        combined[k] = (jnp.stack(base), outs)
        first, second = [got[0], got[1], jnp.max(turned[:16, :128], axis=0)], [outs[1]]
        if k == 0:
            out = reduce_tp(jnp.concatenate(outs))
            combined[k] = combined[k][0].astype(F32) + out
            third = [combined[k]]

    blocks = S * Q
    rel = jnp.array([[r ^ (c * Q) for r in held[h]] for c in range(2) for h in range(2)], jnp.int32)
    place = (rel ^ me)[..., None] == jnp.arange(blocks, dtype=jnp.int32)
    place = place.reshape(2, 2, nb, blocks)
    loss_sum = F32(0)
    head_sum = jnp.zeros((C,), F32)
    grads = [[None, None] for _ in range(K)]
    for k in range(K):
        if k > 0:
            base, outs = combined[k]
            out = reduce_tp(after(jnp.concatenate(outs), local))
            combined[k] = after(base.astype(F32) + out, grads[k - 1][0])
        x = combined[k].reshape(2, 2, nb, sub, C)
        sums = jnp.stack([jnp.sum(x * x, axis=-1), jnp.sum(x * scale, axis=-1)])
        sums = jnp.sum(jnp.where(place[None, ..., None], sums[:, :, :, :, None, :], 0.0), axis=(1, 3))
        square_sum, product_sum = jnp.sum(share(sums, ("section", "phase"), (S, Q), 0), axis=0)
        row_pos = (
            jnp.arange(blocks, dtype=jnp.int32)[None, :, None] * rows
            + ((k * 2 + jnp.arange(2, dtype=jnp.int32)[:, None, None]) * T + t) * sub
            + jnp.arange(sub, dtype=jnp.int32)[None, None, :]
        )
        target, old = returns_at(row_pos.reshape(-1), behavior, frozen, old_values, judge_ratings, lengths)
        target, old = target.reshape(square_sum.shape), old.reshape(square_sum.shape)
        rinv = lax.rsqrt(square_sum / D + EPSILON)
        values = rinv * product_sum
        squash = jnp.tanh((values - old) / CLIP_RANGE)
        clipped = old + CLIP_RANGE * squash
        loss_sum += 0.25 * jnp.sum((values - target) ** 2 + (clipped - target) ** 2)
        dvalue = 0.5 * (values - target) + 0.5 * (clipped - target) * (1.0 - squash * squash)
        rowwise = jnp.stack([rinv, dvalue, values / D])
        rowwise = jnp.sum(
            jnp.where(place[None, ..., None], rowwise[:, None, :, None], 0.0), axis=4
        )[..., None]
        normed = x * rowwise[0]
        head_sum += jnp.sum(normed * rowwise[1], axis=(0, 1, 2, 3))
        g = (rowwise[1] * rowwise[0] * (scale - normed * rowwise[2])).astype(BF16)
        local = g
        g = gather_tp(g.reshape(4 * nb, sub, C)).reshape(2, -1, C)
        grads[k] = [g[0], g[1]]

    hidden_rows = []
    sent = None
    for k in range(K):
        far, near = grads[k][1], grads[k][0]
        if k > 0:
            far, near = after(far, total), after(near, sent)
        far, near = (
            jnp.dot(g, turned, preferred_element_type=F32).reshape(2, nb, piece, FF) for g in (far, near)
        )
        total = near + xchg(far.astype(BF16), "section", 1).astype(F32)
        for h in range(2):
            x = total[h]
            for axis, mask in reversed(orders[h]):
                half = x.shape[0] // 2
                x = x[:half] + xchg(x[half:].astype(BF16), axis, mask).astype(F32)
                if half > 1:
                    sent = x
            hidden_rows.append(x.reshape(piece, FF).astype(BF16))
    hidden_grad = jnp.concatenate(hidden_rows, axis=0)

    all_hidden = jnp.concatenate([pieces[k][c].reshape(-1, FF) for k in range(K) for c in range(2)])
    all_grads = jnp.concatenate([grads[k][c] for k in range(K) for c in range(2)])
    all_grads = after(all_grads, total)
    down_projection_gradient = lax.dot_general(
        all_hidden, all_grads, (((0,), (0,)), ((), ())), preferred_element_type=F32
    )

    packed = after(jnp.concatenate([head_sum, loss_sum[None]]), total)
    packed = share(packed, ("section", "tp"), (S, T), 1).reshape(S, T, -1)
    packed = jnp.sum(packed, axis=1)
    total_loss, head_all = packed[0, -1], packed[:, :-1].reshape(-1)
    return (total_loss, gain * head_all, down_projection_gradient, hidden_grad)


def solution(mesh):
    shape = dict(mesh.shape)
    in_specs = (
        P(("section", "phase"), "tp"),
        P("tp", ("phase", "section")),
        P("section", "phase"),
        P("phase"),
        P("phase"),
        P(),
        P(),
        P(),
        P(),
        P(),
    )
    out_specs = (P(), P("phase"), P("tp", ("phase", "section")), P(("section", "phase"), "tp"))

    def run(*args):
        return on_device(shape, *args)

    return jax.shard_map(run, mesh=mesh, in_specs=in_specs, out_specs=out_specs, check_vma=False)
```

profile of v0, /device:TPU:0, one launch (start us, length us, event | category | flops | bytes accessed | tf_op | source)
XLA Modules:
  0.0 382.5 jit_solution(16345556421247832134)
XLA Ops:
  1.9 3.0 collective-permute-start
  13.8 19.9 %copy.100 = bf16[7168,1024]{0,1:T(8,128)(2,1)} copy(bf16[7168,1024]{1,0:T(8,128)(2,1)} %param.12) | data formatting | bytes 29360128 | tf_op args[1]
  38.5 20.0 %collective-permute-done.1 = bf16[2,32,7168]{2,1,0:T(8,128)(2,1)S(1)} collective-permute-done((bf16[2,32,7168]{2,1,0:T(8,128)(2,1)S(1)}, bf16[2,32,7168]{2,1,0:T(8,128)(2,1)S(1)}, u32[]{:S(2)}, u32[]{:S(2)}) %collective-permute-start.1) | collective-permute-done | bytes 917536 | tf_op jit(solution)/shard_map/ppermute | solution.py:101
  64.9 9.1 %fusion.22 = f32[8,4,8,1024]{3,2,1,0:T(8,128)S(1)} fusion(bf16[8,4,8,7168]{3,2,1,0:T(8,128)(2,1)S(1)} %bitcast.421, bf16[7168,1024]{1,0:T(8,128)(2,1)} %param.12), kind=kOutput, calls=%fused_computation.22 | convolution fusion | flops 3758096384 | bytes 19398656 | tf_op jit(solution)/shard_map/dot_general | solution.py:174
  93.0 6.0 %fusion.20 = f32[8,4,8,1024]{3,2,1,0:T(8,128)S(1)} fusion(bf16[8,4,8,7168]{3,2,1,0:T(8,128)(2,1)} %bitcast.34, bf16[7168,1024]{1,0:T(8,128)(2,1)S(1)} %bitcast.417), kind=kOutput, calls=%fused_computation.20 | convolution fusion | flops 3758096384 | bytes 19398656 | tf_op jit(solution)/shard_map/dot_general | solution.py:174
  104.3 10.1 %collective-permute-done.8 = bf16[16,2,8,1024]{3,2,0,1:T(8,128)(2,1)S(1)} collective-permute-done((bf16[16,2,8,1024]{3,2,0,1:T(8,128)(2,1)S(1)}, bf16[16,2,8,1024]{3,2,0,1:T(8,128)(2,1)S(1)}, u32[]{:S(2)}, u32[]{:S(2)}) %collective-permute-start.8) | collective-permute-done | bytes 524320 | tf_op jit(solution)/shard_map/ppermute | solution.py:101
  119.1 9.9 %collective-permute-done.9 = bf16[16,1,8,1024]{3,2,0,1:T(8,128)(2,1)S(1)} collective-permute-done((bf16[16,1,8,1024]{3,2,0,1:T(8,128)(2,1)S(1)}, bf16[16,1,8,1024]{3,2,0,1:T(8,128)(2,1)S(1)}, u32[]{:S(2)}, u32[]{:S(2)}) %collective-permute-start.9) | collective-permute-done | bytes 262176 | tf_op jit(solution)/shard_map/ppermute | solution.py:101
  131.4 9.7 %shard_map.138 = f32[8,8,128]{2,1,0:T(8,128)} custom-call(f32[8,128]{1,0:T(8,128)} %pad_bitcast_fusion.2.x_ref), custom_call_target="tpu_custom_call" | custom-call | tf_op jit(solution)/shard_map/pallas_call | solution.py:74
  153.3 9.0 %collective-permute-done.17 = bf16[16,1,8,1024]{3,2,0,1:T(8,128)(2,1)S(1)} collective-permute-done((bf16[16,1,8,1024]{3,2,0,1:T(8,128)(2,1)S(1)}, bf16[16,1,8,1024]{3,2,0,1:T(8,128)(2,1)S(1)}, u32[]{:S(2)}, u32[]{:S(2)}) %collective-permute-start.17) | collective-permute-done | bytes 262176 | tf_op jit(solution)/shard_map/ppermute | solution.py:101
  171.9 3.7 collective-permute-done.18
  175.8 10.8 %fusion.24 = bf16[2,4,32,7168]{3,2,1,0:T(8,128)(2,1)} fusion(bf16[2,4,32,1024]{3,2,1,0:T(8,128)(2,1)S(1)} %bitcast.433, bf16[7168,1024]{0,1:T(8,128)(2,1)} %copy.100), kind=kOutput, calls=%fused_computation.24 | convolution fusion | flops 3759931392 | bytes 18874368 | tf_op jit(solution)/shard_map/dot_general | solution.py:238
  186.7 8.7 %fusion.18 = f32[8,2,2,8,1024]{4,3,0,1,2:T(8,128)S(1)} fusion(bf16[7168,1024]{1,0:T(8,128)(2,1)} %param.12, bf16[8,2,2,8,7168]{4,3,2,1,0:T(8,128)(2,1)} %bitcast.108), kind=kOutput, calls=%fused_computation.18 | convolution fusion | flops 3758096384 | bytes 19398656 | tf_op jit(solution)/shard_map/dot_general | solution.py:174
  195.4 6.0 %fusion.16 = f32[8,2,2,8,1024]{4,3,0,1,2:T(8,128)S(1)} fusion(bf16[7168,1024]{1,0:T(8,128)(2,1)S(1)} %bitcast.419, bf16[8,2,2,8,7168]{4,3,2,1,0:T(8,128)(2,1)} %bitcast.110), kind=kOutput, calls=%fused_computation.16 | convolution fusion | flops 3758096384 | bytes 19398656 | tf_op jit(solution)/shard_map/dot_general | solution.py:174
  207.3 9.0 %collective-permute-done.15 = bf16[16,2,8,1024]{3,2,0,1:T(8,128)(2,1)} collective-permute-done((bf16[16,2,8,1024]{3,2,0,1:T(8,128)(2,1)S(1)}, bf16[16,2,8,1024]{3,2,0,1:T(8,128)(2,1)}, u32[]{:S(2)}, u32[]{:S(2)}) %collective-permute-start.15) | collective-permute-done | bytes 524320 | tf_op jit(solution)/shard_map/ppermute | solution.py:101
  218.5 11.9 %fusion.79 = (bf16[2,4,32,7168]{3,2,1,0:T(8,128)(2,1)S(1)}, f32[2,4,32,7168]{3,2,1,0:T(8,128)}) fusion(bf16[2,4,32,7168]{3,2,1,0:T(8,128)(2,1)} %collective-permute-done.21, bf16[2,4,32,1024]{3,2,1,0:T(8,128)(2,1)S(1)} %bitcast.425, bf16[7168,1024]{0,1:T(8,128)(2,1)} %copy.100), kind=kOutput, calls=%fused_computation.272 | convolution fusion | flops 3763601408 | bytes 29884416 | tf_op jit(solution)/shard_map/dot_general | solution.py:238
  234.6 20.9 %shard_map.139 = f32[8,8,128]{2,1,0:T(8,128)} custom-call(f32[8,128]{1,0:T(8,128)} %pad_bitcast_fusion.1.x_ref), custom_call_target="tpu_custom_call" | custom-call | tf_op jit(solution)/shard_map/pallas_call | solution.py:74
  261.6 10.9 %collective-permute-done.19 = bf16[16,1,8,1024]{3,2,0,1:T(8,128)(2,1)S(1)} collective-permute-done((bf16[16,1,8,1024]{3,2,0,1:T(8,128)(2,1)S(1)}, bf16[16,1,8,1024]{3,2,0,1:T(8,128)(2,1)S(1)}, u32[]{:S(2)}, u32[]{:S(2)}) %collective-permute-start.19) | collective-permute-done | bytes 262176 | tf_op jit(solution)/shard_map/ppermute | solution.py:101
  278.9 6.9 %collective-permute-done.20 = bf16[16,2,8,1024]{3,2,0,1:T(8,128)(2,1)S(1)} collective-permute-done((bf16[16,2,8,1024]{3,2,0,1:T(8,128)(2,1)S(1)}, bf16[16,2,8,1024]{3,2,0,1:T(8,128)(2,1)S(1)}, u32[]{:S(2)}, u32[]{:S(2)}) %collective-permute-start.20) | collective-permute-done | bytes 524320 | tf_op jit(solution)/shard_map/ppermute | solution.py:101
  287.0 10.8 %fusion.27 = bf16[2,4,32,7168]{3,2,1,0:T(8,128)(2,1)} fusion(bf16[2,4,32,1024]{3,2,1,0:T(8,128)(2,1)S(1)} %bitcast.437, bf16[7168,1024]{0,1:T(8,128)(2,1)} %copy.100), kind=kOutput, calls=%fused_computation.25 | convolution fusion | flops 3759931392 | bytes 18874368 | tf_op jit(solution)/shard_map/dot_general | solution.py:238
  304.8 7.5 %collective-permute-done.26 = bf16[1,32,7168]{2,1,0:T(8,128)(2,1)S(1)} collective-permute-done((bf16[1,32,7168]{2,1,0:T(8,128)(2,1)S(1)}, bf16[1,32,7168]{2,1,0:T(8,128)(2,1)S(1)}, u32[]{:S(2)}, u32[]{:S(2)}) %collective-permute-start.26) | collective-permute-done | bytes 458784 | tf_op jit(solution)/shard_map/ppermute | solution.py:101
  312.4 10.2 %fusion.77 = (bf16[2,4,32,7168]{3,2,1,0:T(8,128)(2,1)S(1)}, f32[2,4,32,7168]{3,2,1,0:T(8,128)S(1)}) fusion(bf16[2,4,32,7168]{3,2,1,0:T(8,128)(2,1)} %collective-permute-done.23, bf16[2,4,32,1024]{3,2,1,0:T(8,128)(2,1)S(1)} %bitcast.427, bf16[7168,1024]{0,1:T(8,128)(2,1)} %copy.100), kind=kOutput, calls=%fused_computation.271 | convolution fusion | flops 3763601408 | bytes 29884416 | tf_op jit(solution)/shard_map/dot_general | solution.py:238
  327.1 23.3 %fusion = f32[7168,1024]{1,0:T(8,128)} fusion(bf16[256,7168]{1,0:T(8,128)(2,1)} %bitcast.160, bf16[256,7168]{1,0:T(8,128)(2,1)} %bitcast.159, bf16[256,7168]{1,0:T(8,128)(2,1)} %bitcast.158, bf16[256,7168]{1,0:T(8,128)(2,1)} %bitcast.422, bf16[256,1024]{1,0:T(8,128)(2,1)} %bitcast.436, bf16[256,1024]{1,0:T(8,128)(2,1)} %bitcast.435, ...), kind=kOutput, calls=%fused_computation | convolution fusion | flops 15101591552 | bytes 46137344 | tf_op jit(solution)/shard_map/dot_general | solution.py:254
  356.6 9.1 %shard_map.140 = f32[16,16,128]{2,1,0:T(8,128)} custom-call(f32[16,128]{1,0:T(8,128)} %pad_bitcast_fusion.x_ref), custom_call_target="tpu_custom_call" | custom-call | tf_op jit(solution)/shard_map/pallas_call | solution.py:74
  371.0 9.7 %collective-permute-done.30 = bf16[1,32,7168]{2,1,0:T(8,128)(2,1)S(1)} collective-permute-done((bf16[1,32,7168]{2,1,0:T(8,128)(2,1)S(1)}, bf16[1,32,7168]{2,1,0:T(8,128)(2,1)S(1)}, u32[]{:S(2)}, u32[]{:S(2)}) %collective-permute-start.30) | collective-permute-done | bytes 458784 | tf_op jit(solution)/shard_map/ppermute | solution.py:101
  (306 shorter events, 113.0 us)
Async XLA Ops:
  1.9 33.9 %collective-permute-start = (bf16[1,32,7168]{2,1,0:T(8,128)(2,1)S(1)}, bf16[1,32,7168]{2,1,0:T(8,128)(2,1)}, u32[]{:S(2)}, u32[]{:S(2)}) collective-permute-start(bf16[1,32,7168]{2,1,0:T(8,128)(2,1)S(1)} %get-tuple-element.39), channel_id=1, source_target_pairs={{0,4},{4,0},{1,5},{5,1},{2,6},{6,2},{3,7},{7,3},{8,12},{12,8},{9,1... | collective-permute-start | bytes 1376264 | tf_op jit(solution)/shard_map/ppermute | solution.py:101
  4.9 33.4 %collective-permute-start.5 = (bf16[1,32,7168]{2,1,0:T(8,128)(2,1)S(1)}, bf16[1,32,7168]{2,1,0:T(8,128)(2,1)S(1)}, u32[]{:S(2)}, u32[]{:S(2)}) collective-permute-start(bf16[1,32,7168]{2,1,0:T(8,128)(2,1)S(1)} %get-tuple-element.38), channel_id=1, source_target_pairs={{0,16},{8,24},{16,0},{24,8},{1,17},{9,25},{17,1},{25,9},{2,18},{10... | collective-permute-start | bytes 1376264 | tf_op jit(solution)/shard_map/ppermute | solution.py:101
  36.9 21.6 %collective-permute-start.1 = (bf16[2,32,7168]{2,1,0:T(8,128)(2,1)S(1)}, bf16[2,32,7168]{2,1,0:T(8,128)(2,1)S(1)}, u32[]{:S(2)}, u32[]{:S(2)}) collective-permute-start(bf16[2,32,7168]{2,1,0:T(8,128)(2,1)S(1)} %pad_maximum_fusion.3), channel_id=1, source_target_pairs={{0,16},{8,24},{16,0},{24,8},{1,17},{9,25},{17,1},{25,9},{2,18},{10... | collective-permute-start | bytes 2752520 | tf_op jit(solution)/shard_map/ppermute | solution.py:101
  38.3 25.9 %collective-permute-start.6 = (bf16[2,32,7168]{2,1,0:T(8,128)(2,1)S(1)}, bf16[2,32,7168]{2,1,0:T(8,128)(2,1)S(1)}, u32[]{:S(2)}, u32[]{:S(2)}) collective-permute-start(bf16[2,32,7168]{2,1,0:T(8,128)(2,1)S(1)} %pad_maximum_fusion.4), channel_id=1, source_target_pairs={{0,4},{4,0},{1,5},{5,1},{2,6},{6,2},{3,7},{7,3},{8,12},{12,8},{9,1... | collective-permute-start | bytes 2752520 | tf_op jit(solution)/shard_map/ppermute | solution.py:101
  60.8 15.3 %collective-permute-start.2 = (bf16[2,2,2,8,1024]{4,3,2,1,0:T(8,128)(2,1)S(1)}, bf16[2,2,2,8,1024]{4,3,2,1,0:T(8,128)(2,1)S(1)}, u32[]{:S(2)}, u32[]{:S(2)}) collective-permute-start(bf16[2,2,2,8,1024]{4,3,2,1,0:T(8,128)(2,1)S(1)} %get-tuple-element.58), channel_id=1, source_target_pairs={{0,16},{8,24},{16,0},{24,8},{1,17},{9,25},{17,1},{25,9},{2,18},{10... | collective-permute-start | bytes 393224 | tf_op jit(solution)/shard_map/ppermute | solution.py:101
  61.3 22.3 %collective-permute-start.3 = (bf16[2,2,2,8,1024]{4,3,2,1,0:T(8,128)(2,1)}, bf16[2,2,2,8,1024]{4,3,2,1,0:T(8,128)(2,1)S(1)}, u32[]{:S(2)}, u32[]{:S(2)}) collective-permute-start(bf16[2,2,2,8,1024]{4,3,2,1,0:T(8,128)(2,1)} %get-tuple-element.57), channel_id=1, source_target_pairs={{0,8},{8,0},{16,24},{24,16},{1,9},{9,1},{17,25},{25,17},{2,10},{10... | collective-permute-start | bytes 393224 | tf_op jit(solution)/shard_map/ppermute | solution.py:101
  61.4 22.3 %collective-permute-start.4 = (bf16[2,2,2,8,1024]{4,3,2,1,0:T(8,128)(2,1)}, bf16[2,2,2,8,1024]{4,3,2,1,0:T(8,128)(2,1)}, u32[]{:S(2)}, u32[]{:S(2)}) collective-permute-start(bf16[2,2,2,8,1024]{4,3,2,1,0:T(8,128)(2,1)} %get-tuple-element.56), channel_id=1, source_target_pairs={{0,24},{8,16},{16,8},{24,0},{1,25},{9,17},{17,9},{25,1},{2,26},{10... | collective-permute-start | bytes 393224 | tf_op jit(solution)/shard_map/ppermute | solution.py:101
  64.8 28.2 %collective-permute-start.7 = (bf16[2,4,32,7168]{3,2,1,0:T(8,128)(2,1)S(1)}, bf16[2,4,32,7168]{3,2,1,0:T(8,128)(2,1)}, u32[]{:S(2)}, u32[]{:S(2)}) collective-permute-start(bf16[2,4,32,7168]{3,2,1,0:T(8,128)(2,1)S(1)} %pad_maximum_fusion), channel_id=1, source_target_pairs={{0,8},{8,0},{16,24},{24,16},{1,9},{9,1},{17,25},{25,17},{2,10},{10... | collective-permute-start | bytes 11010056 | tf_op jit(solution)/shard_map/ppermute | solution.py:101
  75.5 27.1 %collective-permute-start.10 = (bf16[1,32,7168]{2,1,0:T(8,128)(2,1)S(1)}, bf16[1,32,7168]{2,1,0:T(8,128)(2,1)S(1)}, u32[]{:S(2)}, u32[]{:S(2)}) collective-permute-start(bf16[1,32,7168]{2,1,0:T(8,128)(2,1)S(1)} %get-tuple-element.36), channel_id=1, source_target_pairs={{0,4},{4,0},{1,5},{5,1},{2,6},{6,2},{3,7},{7,3},{8,12},{12,8},{9,1... | collective-permute-start | bytes 1376264 | tf_op jit(solution)/shard_map/ppermute | solution.py:101
  76.7 40.7 %collective-permute-start.12 = (bf16[1,32,7168]{2,1,0:T(8,128)(2,1)S(1)}, bf16[1,32,7168]{2,1,0:T(8,128)(2,1)S(1)}, u32[]{:S(2)}, u32[]{:S(2)}) collective-permute-start(bf16[1,32,7168]{2,1,0:T(8,128)(2,1)S(1)} %get-tuple-element.37), channel_id=1, source_target_pairs={{0,16},{8,24},{16,0},{24,8},{1,17},{9,25},{17,1},{25,9},{2,18},{10... | collective-permute-start | bytes 1376264 | tf_op jit(solution)/shard_map/ppermute | solution.py:101
  102.7 47.0 %collective-permute-start.11 = (bf16[2,32,7168]{2,1,0:T(8,128)(2,1)S(1)}, bf16[2,32,7168]{2,1,0:T(8,128)(2,1)S(1)}, u32[]{:S(2)}, u32[]{:S(2)}) collective-permute-start(bf16[2,32,7168]{2,1,0:T(8,128)(2,1)S(1)} %maximum_add_fusion.4), channel_id=1, source_target_pairs={{0,16},{8,24},{16,0},{24,8},{1,17},{9,25},{17,1},{25,9},{2,18},{10... | collective-permute-start | bytes 2752520 | tf_op jit(solution)/shard_map/ppermute | solution.py:101
  117.5 32.3 %collective-permute-start.13 = (bf16[2,32,7168]{2,1,0:T(8,128)(2,1)S(1)}, bf16[2,32,7168]{2,1,0:T(8,128)(2,1)}, u32[]{:S(2)}, u32[]{:S(2)}) collective-permute-start(bf16[2,32,7168]{2,1,0:T(8,128)(2,1)S(1)} %maximum_add_fusion.5), channel_id=1, source_target_pairs={{0,4},{4,0},{1,5},{5,1},{2,6},{6,2},{3,7},{7,3},{8,12},{12,8},{9,1... | collective-permute-start | bytes 2752520 | tf_op jit(solution)/shard_map/ppermute | solution.py:101
  147.5 14.8 %collective-permute-start.17 = (bf16[16,1,8,1024]{3,2,0,1:T(8,128)(2,1)S(1)}, bf16[16,1,8,1024]{3,2,0,1:T(8,128)(2,1)S(1)}, u32[]{:S(2)}, u32[]{:S(2)}) collective-permute-start(bf16[16,1,8,1024]{3,2,0,1:T(8,128)(2,1)S(1)} %get-tuple-element.49), channel_id=1, source_target_pairs={{0,2},{1,3},{2,0},{3,1},{4,6},{5,7},{6,4},{7,5},{8,10},{9,11},{10,... | collective-permute-start | bytes 786440 | tf_op jit(solution)/shard_map/ppermute | solution.py:101
  153.3 42.0 %collective-permute-start.14 = (bf16[2,4,32,7168]{3,2,1,0:T(8,128)(2,1)}, bf16[2,4,32,7168]{3,2,1,0:T(8,128)(2,1)}, u32[]{:S(2)}, u32[]{:S(2)}) collective-permute-start(bf16[2,4,32,7168]{3,2,1,0:T(8,128)(2,1)} %maximum_add_fusion), channel_id=1, source_target_pairs={{0,8},{8,0},{16,24},{24,16},{1,9},{9,1},{17,25},{25,17},{2,10},{10... | collective-permute-start | bytes 11010056 | tf_op jit(solution)/shard_map/ppermute | solution.py:101
  186.6 31.9 %collective-permute-start.21 = (bf16[2,4,32,7168]{3,2,1,0:T(8,128)(2,1)}, bf16[2,4,32,7168]{3,2,1,0:T(8,128)(2,1)}, u32[]{:S(2)}, u32[]{:S(2)}) collective-permute-start(bf16[2,4,32,7168]{3,2,1,0:T(8,128)(2,1)} %fusion.24), channel_id=1, source_target_pairs={{0,8},{8,0},{16,24},{24,16},{1,9},{9,1},{17,25},{25,17},{2,10},{10... | collective-permute-start | bytes 11010056 | tf_op jit(solution)/shard_map/ppermute | solution.py:101
  201.8 14.5 %collective-permute-start.15 = (bf16[16,2,8,1024]{3,2,0,1:T(8,128)(2,1)S(1)}, bf16[16,2,8,1024]{3,2,0,1:T(8,128)(2,1)}, u32[]{:S(2)}, u32[]{:S(2)}) collective-permute-start(bf16[16,2,8,1024]{3,2,0,1:T(8,128)(2,1)S(1)} %fusion.50), channel_id=1, source_target_pairs={{0,1},{1,0},{2,3},{3,2},{4,5},{5,4},{6,7},{7,6},{8,9},{9,8},{10,11... | collective-permute-start | bytes 1572872 | tf_op jit(solution)/shard_map/ppermute | solution.py:101
  217.6 15.9 %collective-permute-start.16 = (bf16[16,1,8,1024]{3,2,0,1:T(8,128)(2,1)S(1)}, bf16[16,1,8,1024]{3,2,0,1:T(8,128)(2,1)S(1)}, u32[]{:S(2)}, u32[]{:S(2)}) collective-permute-start(bf16[16,1,8,1024]{3,2,0,1:T(8,128)(2,1)S(1)} %fusion.72), channel_id=1, source_target_pairs={{0,2},{1,3},{2,0},{3,1},{4,6},{5,7},{6,4},{7,5},{8,10},{9,11},{10,... | collective-permute-start | bytes 786440 | tf_op jit(solution)/shard_map/ppermute | solution.py:101
  231.5 41.2 %collective-permute-start.22 = (bf16[2,32,7168]{2,1,0:T(8,128)(2,1)}, bf16[2,32,7168]{2,1,0:T(8,128)(2,1)S(1)}, u32[]{:S(2)}, u32[]{:S(2)}) collective-permute-start(bf16[2,32,7168]{2,1,0:T(8,128)(2,1)} %get-tuple-element.31), channel_id=1, source_target_pairs={{0,4},{4,0},{1,5},{5,1},{2,6},{6,2},{3,7},{7,3},{8,12},{12,8},{9,1... | collective-permute-start | bytes 2752520 | tf_op jit(solution)/shard_map/ppermute | solution.py:101
  233.0 39.7 %collective-permute-start.24 = (bf16[2,32,7168]{2,1,0:T(8,128)(2,1)S(1)}, bf16[2,32,7168]{2,1,0:T(8,128)(2,1)}, u32[]{:S(2)}, u32[]{:S(2)}) collective-permute-start(bf16[2,32,7168]{2,1,0:T(8,128)(2,1)S(1)} %get-tuple-element.30), channel_id=1, source_target_pairs={{0,16},{8,24},{16,0},{24,8},{1,17},{9,25},{17,1},{25,9},{2,18},{10... | collective-permute-start | bytes 2752520 | tf_op jit(solution)/shard_map/ppermute | solution.py:101
  257.6 14.9 %collective-permute-start.19 = (bf16[16,1,8,1024]{3,2,0,1:T(8,128)(2,1)S(1)}, bf16[16,1,8,1024]{3,2,0,1:T(8,128)(2,1)S(1)}, u32[]{:S(2)}, u32[]{:S(2)}) collective-permute-start(bf16[16,1,8,1024]{3,2,0,1:T(8,128)(2,1)S(1)} %get-tuple-element.50), channel_id=1, source_target_pairs={{0,2},{1,3},{2,0},{3,1},{4,6},{5,7},{6,4},{7,5},{8,10},{9,11},{10,... | collective-permute-start | bytes 786440 | tf_op jit(solution)/shard_map/ppermute | solution.py:101
  277.4 26.3 %collective-permute-start.25 = (bf16[1,32,7168]{2,1,0:T(8,128)(2,1)}, bf16[1,32,7168]{2,1,0:T(8,128)(2,1)}, u32[]{:S(2)}, u32[]{:S(2)}) collective-permute-start(bf16[1,32,7168]{2,1,0:T(8,128)(2,1)} %slice.741), channel_id=1, source_target_pairs={{0,4},{4,0},{1,5},{5,1},{2,6},{6,2},{3,7},{7,3},{8,12},{12,8},{9,1... | collective-permute-start | bytes 1376264 | tf_op jit(solution)/shard_map/ppermute | solution.py:101
  297.9 14.5 %collective-permute-start.23 = (bf16[2,4,32,7168]{3,2,1,0:T(8,128)(2,1)}, bf16[2,4,32,7168]{3,2,1,0:T(8,128)(2,1)}, u32[]{:S(2)}, u32[]{:S(2)}) collective-permute-start(bf16[2,4,32,7168]{3,2,1,0:T(8,128)(2,1)} %fusion.27), channel_id=1, source_target_pairs={{0,8},{8,0},{16,24},{24,16},{1,9},{9,1},{17,25},{25,17},{2,10},{10... | collective-permute-start | bytes 11010056 | tf_op jit(solution)/shard_map/ppermute | solution.py:101
  323.9 26.5 %collective-permute-start.27 = (bf16[2,32,7168]{2,1,0:T(8,128)(2,1)}, bf16[2,32,7168]{2,1,0:T(8,128)(2,1)S(1)}, u32[]{:S(2)}, u32[]{:S(2)}) collective-permute-start(bf16[2,32,7168]{2,1,0:T(8,128)(2,1)} %get-tuple-element.32), channel_id=1, source_target_pairs={{0,16},{8,24},{16,0},{24,8},{1,17},{9,25},{17,1},{25,9},{2,18},{10... | collective-permute-start | bytes 2752520 | tf_op jit(solution)/shard_map/ppermute | solution.py:101
  324.3 26.9 %collective-permute-start.29 = (bf16[2,32,7168]{2,1,0:T(8,128)(2,1)S(1)}, bf16[2,32,7168]{2,1,0:T(8,128)(2,1)}, u32[]{:S(2)}, u32[]{:S(2)}) collective-permute-start(bf16[2,32,7168]{2,1,0:T(8,128)(2,1)S(1)} %get-tuple-element.33), channel_id=1, source_target_pairs={{0,4},{4,0},{1,5},{5,1},{2,6},{6,2},{3,7},{7,3},{8,12},{12,8},{9,1... | collective-permute-start | bytes 2752520 | tf_op jit(solution)/shard_map/ppermute | solution.py:101
  (41 other events, 587.4 us)
where the time goes:
time: 390 us; the launch traced here: 382 us
  matrix products  96.8 us (25%)
  waiting for transfers between devices  96.7 us (25%)
  local copies, waits for them, and re-layouts  76.6 us (20%)
  Pallas kernels  39.7 us (10%)
  other arithmetic  32.2 us (8%)
  starting transfers between devices  27.1 us (7%)
  between operations  13.3 us (3%)
    ppermute x31, waiting for transfers between devices, xchg(): return lax.ppermute(x, axis, [(i, i ^ mask) for i in range(sizes[axis])])  96.7 us
    unnamed x118, local copies, waits for them, and re-layouts  45.7 us
    dot_general x4, matrix products, on_device(): jnp.dot(g, turned, preferred_element_type=F32).reshape(2, nb, piece, FF)  43.8 us
    pallas_call x3, Pallas kernels, share(): pl.pallas_call(functools.partial(exchange_kernel, axes, sizes), out_shape...  39.7 us
    dot_general x4, matrix products, on_device(): jnp.dot(pieces[k][c].reshape(-1, FF), down_weight, preferred_element_type...  29.8 us
    ppermute x31, starting transfers between devices, xchg(): return lax.ppermute(x, axis, [(i, i ^ mask) for i in range(sizes[axis])])  27.1 us
    dot_general x1, matrix products, on_device(): lax.dot_general(all_hidden, all_grads, (((0,), (0,)), ((), ())), preferre...  23.3 us
    slice x15, local copies, waits for them, and re-layouts, after(): x = x + (0 * y[(0,) * y.ndim]).astype(x.dtype)  8.81 us
  transfers between devices with their start and end apart: 31, of which 10 were waited for; matrix products, arithmetic and copies ran while one was open for 48% of the time, Pallas kernels for 10%

commit v1 on v0

--- a/solution.py
+++ b/solution.py
@@ -130,7 +130,7 @@
         for m in range(S):
             part = lax.dynamic_index_in_dim(res, s ^ m, 4, keepdims=False)
             res_by.append(part if m == 0 else xchg(part, "section", m))
-        return res_by
+        return jnp.stack(res_by).reshape(S // 2, 2, Q, K, 2, sub, C)
 
     def reduce_tp(x):
         n, bit = T, 1
@@ -155,16 +155,18 @@
         return x
 
     scale = lax.dynamic_slice_in_dim(gain * head_weight, s * C, C, 0)
-    turned = with_layout_constraint(down_weight.T, Layout((0, 1)))
     pieces = [None] * K
     combined = [None] * K
-    first, second, third = [], [], []
+    products = [None] * K
+    second, third = [], []
     for k in range(K):
-        cur = [after(own[k, h], *first) for h in range(2)]
+        cur = [own[k, h] for h in range(2)]
         for j in range(len(orders[0])):
             got = [xchg(cur[h], *orders[h][j]) for h in range(2)]
             cur = [jnp.concatenate([cur[h], got[h]], axis=0) for h in range(2)]
             if j == 0:
+                if k == 0:
+                    turned = with_layout_constraint(down_weight.T, Layout((0, 1)))
                 cur = [after(x, *second) for x in cur]
         here = after(jnp.stack(cur), *third)
         pieces[k] = [here, xchg(here, "section", 1)]
@@ -175,14 +177,13 @@
             .reshape(2 * nb, T, sub, C)
             for c in range(2)
         ]
-        base = []
-        for c in range(2):
-            for h in range(2):
-                for r in held[h]:
-                    rr = r ^ (c * Q)
-                    base.append(res_by[rr // Q][rr % Q, k, h])
-        combined[k] = (jnp.stack(base), outs)
-        first, second = [got[0], got[1], jnp.max(turned[:16, :128], axis=0)], [outs[1]]
+        base = jnp.stack([
+            jnp.transpose(res_by[:, :, :, k, 0], (1, 0, 2, 3, 4)).reshape(2, nb, sub, C),
+            jnp.transpose(res_by[:, :, :, k, 1], (1, 2, 0, 3, 4)).reshape(2, nb, sub, C),
+        ], axis=1).reshape(4 * nb, sub, C)
+        combined[k] = (base, outs)
+        products[k] = outs
+        second = [got[0], got[1], outs[0], jnp.max(turned[:16, :128], axis=0)]
         if k == 0:
             out = reduce_tp(jnp.concatenate(outs))
             combined[k] = combined[k][0].astype(F32) + out
@@ -198,7 +199,7 @@
     for k in range(K):
         if k > 0:
             base, outs = combined[k]
-            out = reduce_tp(after(jnp.concatenate(outs), local))
+            out = reduce_tp(jnp.concatenate(outs))
             combined[k] = after(base.astype(F32) + out, grads[k - 1][0])
         x = combined[k].reshape(2, 2, nb, sub, C)
         sums = jnp.stack([jnp.sum(x * x, axis=-1), jnp.sum(x * scale, axis=-1)])
@@ -224,7 +225,6 @@
         normed = x * rowwise[0]
         head_sum += jnp.sum(normed * rowwise[1], axis=(0, 1, 2, 3))
         g = (rowwise[1] * rowwise[0] * (scale - normed * rowwise[2])).astype(BF16)
-        local = g
         g = gather_tp(g.reshape(4 * nb, sub, C)).reshape(2, -1, C)
         grads[k] = [g[0], g[1]]
 
@@ -232,6 +232,8 @@
     sent = None
     for k in range(K):
         far, near = grads[k][1], grads[k][0]
+        if k + 1 < K:
+            far = after(far, products[k + 1][1])
         if k > 0:
             far, near = after(far, total), after(near, sent)
         far, near = (

time: 390 us -> 343 us (0.88)
  local copies, waits for them, and re-layouts: 76.6 us -> 45.4 us
  waiting for transfers between devices: 96.7 us -> 120 us
  Pallas kernels: 39.7 us -> 22.2 us
  matrix products: 96.8 us -> 85.8 us
  other arithmetic: 32.2 us -> 25.1 us
    ppermute x31, waiting for transfers between devices: 96.7 us -> 120 us  [xchg(): return lax.ppermute(x, axis, [(i, i ^ mask) for i in range(sizes[axis])])]
    unnamed x118 -> x61, local copies, waits for them, and re-layouts: 45.7 us -> 26.4 us
    pallas_call x3, Pallas kernels: 39.7 us -> 22.2 us  [share(): pl.pallas_call(functools.partial(exchange_kernel, axes, sizes), out_shape...]
    dot_general x4, matrix products: 43.8 us -> 32.1 us  [on_device(): jnp.dot(g, turned, preferred_element_type=F32).reshape(2, nb, piece, FF)]
    slice x15 -> x10, local copies, waits for them, and re-layouts: 8.81 us -> 5.21 us  [after(): x = x + (0 * y[(0,) * y.ndim]).astype(x.dtype)]
  transfers between devices with their start and end apart: 31 -> 31, of which waited for: 10 -> 15; matrix products, arithmetic and copies ran while one was open for 48% -> 34% of each run, Pallas kernels for 10% -> 7%
where the time goes in v1:
time: 343 us; the launch traced here: 338 us
  waiting for transfers between devices  120 us (35%)
  matrix products  85.8 us (25%)
  local copies, waits for them, and re-layouts  45.4 us (13%)
  starting transfers between devices  28.2 us (8%)
  other arithmetic  25.1 us (7%)
  Pallas kernels  22.2 us (6%)
  between operations  10.7 us (3%)
    ppermute x31, waiting for transfers between devices, xchg(): return lax.ppermute(x, axis, [(i, i ^ mask) for i in range(sizes[axis])])  120 us
    dot_general x4, matrix products, on_device(): jnp.dot(g, turned, preferred_element_type=F32).reshape(2, nb, piece, FF)  32.1 us
    dot_general x4, matrix products, on_device(): jnp.dot(pieces[k][c].reshape(-1, FF), down_weight, preferred_element_type...  30.5 us
    ppermute x31, starting transfers between devices, xchg(): return lax.ppermute(x, axis, [(i, i ^ mask) for i in range(sizes[axis])])  28.2 us
    unnamed x61, local copies, waits for them, and re-layouts  26.4 us
    dot_general x1, matrix products, on_device(): lax.dot_general(all_hidden, all_grads, (((0,), (0,)), ((), ())), preferre...  23.2 us
    pallas_call x3, Pallas kernels, share(): pl.pallas_call(functools.partial(exchange_kernel, axes, sizes), out_shape...  22.2 us
  transfers between devices with their start and end apart: 31, of which 15 were waited for; matrix products, arithmetic and copies ran while one was open for 34% of the time, Pallas kernels for 7%

profile of v1, /device:TPU:0, one launch (start us, length us, event | category | flops | bytes accessed | tf_op | source)
XLA Modules:
  0.0 337.8 jit_solution(10516977293532586896)
XLA Ops:
  2.2 3.0 collective-permute-start
  8.4 19.9 %copy.81 = bf16[7168,1024]{0,1:T(8,128)(2,1)} copy(bf16[7168,1024]{1,0:T(8,128)(2,1)} %param.12) | data formatting | bytes 29360128 | tf_op args[1]
  34.8 16.9 %collective-permute-done.6 = bf16[2,32,7168]{2,1,0:T(8,128)(2,1)S(1)} collective-permute-done((bf16[2,32,7168]{2,1,0:T(8,128)(2,1)S(1)}, bf16[2,32,7168]{2,1,0:T(8,128)(2,1)S(1)}, u32[]{:S(2)}, u32[]{:S(2)}) %collective-permute-start.6) | collective-permute-done | bytes 917536 | tf_op jit(solution)/shard_map/ppermute | solution.py:101
  57.7 7.6 %fusion.22 = f32[8,4,8,1024]{3,2,1,0:T(8,128)S(1)} fusion(bf16[8,4,8,7168]{3,2,1,0:T(8,128)(2,1)S(1)} %bitcast.275, bf16[7168,1024]{1,0:T(8,128)(2,1)} %param.12), kind=kOutput, calls=%fused_computation.22 | convolution fusion | flops 3758096384 | bytes 19398656 | tf_op jit(solution)/shard_map/dot_general | solution.py:176
  72.7 6.0 %fusion.20 = f32[8,4,8,1024]{3,2,1,0:T(8,128)S(1)} fusion(bf16[8,4,8,7168]{3,2,1,0:T(8,128)(2,1)} %bitcast.28, bf16[7168,1024]{1,0:T(8,128)(2,1)S(1)} %bitcast.272), kind=kOutput, calls=%fused_computation.20 | convolution fusion | flops 3758096384 | bytes 19398656 | tf_op jit(solution)/shard_map/dot_general | solution.py:176
  80.8 11.1 %collective-permute-done.11 = bf16[2,32,7168]{2,1,0:T(8,128)(2,1)S(1)} collective-permute-done((bf16[2,32,7168]{2,1,0:T(8,128)(2,1)S(1)}, bf16[2,32,7168]{2,1,0:T(8,128)(2,1)S(1)}, u32[]{:S(2)}, u32[]{:S(2)}) %collective-permute-start.11) | collective-permute-done | bytes 917536 | tf_op jit(solution)/shard_map/ppermute | solution.py:101
  95.7 10.7 %collective-permute-done.9 = bf16[16,1,8,1024]{3,2,0,1:T(8,128)(2,1)S(1)} collective-permute-done((bf16[16,1,8,1024]{3,2,0,1:T(8,128)(2,1)S(1)}, bf16[16,1,8,1024]{3,2,0,1:T(8,128)(2,1)S(1)}, u32[]{:S(2)}, u32[]{:S(2)}) %collective-permute-start.9) | collective-permute-done | bytes 262176 | tf_op jit(solution)/shard_map/ppermute | solution.py:101
  111.3 6.4 %shard_map.138 = f32[8,8,128]{2,1,0:T(8,128)} custom-call(f32[8,128]{1,0:T(8,128)} %pad_bitcast_fusion.2.x_ref), custom_call_target="tpu_custom_call" | custom-call | tf_op jit(solution)/shard_map/pallas_call | solution.py:74
  119.8 14.9 %collective-permute-done.17 = bf16[16,1,8,1024]{3,2,0,1:T(8,128)(2,1)S(1)} collective-permute-done((bf16[16,1,8,1024]{3,2,0,1:T(8,128)(2,1)S(1)}, bf16[16,1,8,1024]{3,2,0,1:T(8,128)(2,1)S(1)}, u32[]{:S(2)}, u32[]{:S(2)}) %collective-permute-start.17) | collective-permute-done | bytes 262176 | tf_op jit(solution)/shard_map/ppermute | solution.py:101
  134.8 8.4 %fusion.18 = f32[8,4,8,1024]{3,2,1,0:T(8,128)S(1)} fusion(bf16[8,4,8,7168]{3,2,1,0:T(8,128)(2,1)} %bitcast.63, bf16[7168,1024]{1,0:T(8,128)(2,1)} %param.12), kind=kOutput, calls=%fused_computation.18 | convolution fusion | flops 3758096384 | bytes 19398656 | tf_op jit(solution)/shard_map/dot_general | solution.py:176
  143.3 4.7 %collective-permute-done.18 = bf16[16,2,8,1024]{3,2,0,1:T(8,128)(2,1)S(1)} collective-permute-done((bf16[16,2,8,1024]{3,2,0,1:T(8,128)(2,1)S(1)}, bf16[16,2,8,1024]{3,2,0,1:T(8,128)(2,1)S(1)}, u32[]{:S(2)}, u32[]{:S(2)}) %collective-permute-start.18) | collective-permute-done | bytes 524320 | tf_op jit(solution)/shard_map/ppermute | solution.py:101
  148.1 8.5 %fusion.16 = f32[8,4,8,1024]{3,2,1,0:T(8,128)S(1)} fusion(bf16[8,4,8,7168]{3,2,1,0:T(8,128)(2,1)} %bitcast.64, bf16[7168,1024]{1,0:T(8,128)(2,1)} %param.12), kind=kOutput, calls=%fused_computation.16 | convolution fusion | flops 3758096384 | bytes 19398656 | tf_op jit(solution)/shard_map/dot_general | solution.py:176
  158.5 5.7 %fusion.24 = bf16[2,4,32,7168]{3,2,1,0:T(8,128)(2,1)} fusion(bf16[2,4,32,1024]{3,2,1,0:T(8,128)(2,1)S(1)} %bitcast.290, bf16[7168,1024]{0,1:T(8,128)(2,1)S(1)} %bitcast.268), kind=kOutput, calls=%fused_computation.24 | convolution fusion | flops 3759931392 | bytes 18874368 | tf_op jit(solution)/shard_map/dot_general | solution.py:240
  165.1 14.0 %collective-permute-done.15 = bf16[16,2,8,1024]{3,2,0,1:T(8,128)(2,1)S(1)} collective-permute-done((bf16[16,2,8,1024]{3,2,0,1:T(8,128)(2,1)S(1)}, bf16[16,2,8,1024]{3,2,0,1:T(8,128)(2,1)S(1)}, u32[]{:S(2)}, u32[]{:S(2)}) %collective-permute-start.15) | collective-permute-done | bytes 524320 | tf_op jit(solution)/shard_map/ppermute | solution.py:101
  182.5 12.1 %collective-permute-done.16 = bf16[16,1,8,1024]{3,2,0,1:T(8,128)(2,1)S(1)} collective-permute-done((bf16[16,1,8,1024]{3,2,0,1:T(8,128)(2,1)}, bf16[16,1,8,1024]{3,2,0,1:T(8,128)(2,1)S(1)}, u32[]{:S(2)}, u32[]{:S(2)}) %collective-permute-start.16) | collective-permute-done | bytes 262176 | tf_op jit(solution)/shard_map/ppermute | solution.py:101
  195.6 6.1 %shard_map.139 = f32[8,8,128]{2,1,0:T(8,128)} custom-call(f32[8,128]{1,0:T(8,128)} %pad_bitcast_fusion.1.x_ref), custom_call_target="tpu_custom_call" | custom-call | tf_op jit(solution)/shard_map/pallas_call | solution.py:74
  204.5 10.4 %fusion.79 = (bf16[2,4,32,7168]{3,2,1,0:T(8,128)(2,1)S(1)}, f32[2,4,32,7168]{3,2,1,0:T(8,128)S(1)}) fusion(bf16[2,4,32,7168]{3,2,1,0:T(8,128)(2,1)} %collective-permute-done.21, bf16[2,4,32,1024]{3,2,1,0:T(8,128)(2,1)S(1)} %bitcast.279, bf16[7168,1024]{0,1:T(8,128)(2,1)} %copy.81), kind=kOutput, calls=%fused_computation.212 | convolution fusion | flops 3763601408 | bytes 29884416 | tf_op jit(solution)/shard_map/dot_general | solution.py:240
  220.8 13.2 %collective-permute-done.20 = bf16[16,2,8,1024]{3,2,0,1:T(8,128)(2,1)S(1)} collective-permute-done((bf16[16,2,8,1024]{3,2,0,1:T(8,128)(2,1)S(1)}, bf16[16,2,8,1024]{3,2,0,1:T(8,128)(2,1)S(1)}, u32[]{:S(2)}, u32[]{:S(2)}) %collective-permute-start.20) | collective-permute-done | bytes 524320 | tf_op jit(solution)/shard_map/ppermute | solution.py:101
  244.3 5.8 %fusion.27 = bf16[2,4,32,7168]{3,2,1,0:T(8,128)(2,1)} fusion(bf16[2,4,32,1024]{3,2,1,0:T(8,128)(2,1)S(1)} %bitcast.291, bf16[7168,1024]{0,1:T(8,128)(2,1)S(1)} %bitcast.270), kind=kOutput, calls=%fused_computation.25 | convolution fusion | flops 3759931392 | bytes 18874368 | tf_op jit(solution)/shard_map/dot_general | solution.py:240
  259.8 5.5 %collective-permute-done.26 = bf16[1,32,7168]{2,1,0:T(8,128)(2,1)S(1)} collective-permute-done((bf16[1,32,7168]{2,1,0:T(8,128)(2,1)S(1)}, bf16[1,32,7168]{2,1,0:T(8,128)(2,1)S(1)}, u32[]{:S(2)}, u32[]{:S(2)}) %collective-permute-start.26) | collective-permute-done | bytes 458784 | tf_op jit(solution)/shard_map/ppermute | solution.py:101
  266.2 10.2 %fusion.77 = (bf16[2,4,32,7168]{3,2,1,0:T(8,128)(2,1)S(1)}, f32[2,4,32,7168]{3,2,1,0:T(8,128)S(1)}) fusion(bf16[2,4,32,7168]{3,2,1,0:T(8,128)(2,1)} %collective-permute-done.23, bf16[2,4,32,1024]{3,2,1,0:T(8,128)(2,1)S(1)} %bitcast.281, bf16[7168,1024]{0,1:T(8,128)(2,1)} %copy.81), kind=kOutput, calls=%fused_computation.211 | convolution fusion | flops 3763601408 | bytes 29884416 | tf_op jit(solution)/shard_map/dot_general | solution.py:240
  280.9 23.2 %fusion = f32[7168,1024]{1,0:T(8,128)} fusion(bf16[256,7168]{1,0:T(8,128)(2,1)} %bitcast.110, bf16[256,7168]{1,0:T(8,128)(2,1)} %bitcast.109, bf16[256,7168]{1,0:T(8,128)(2,1)} %bitcast.108, bf16[256,7168]{1,0:T(8,128)(2,1)} %bitcast.276, bf16[256,1024]{1,0:T(8,128)(2,1)} %bitcast.289, bf16[256,1024]{1,0:T(8,128)(2,1)} %bitcast.288, ...), kind=kOutput, calls=%fused_computation | convolution fusion | flops 15101591552 | bytes 46137344 | tf_op jit(solution)/shard_map/dot_general | solution.py:256
  311.3 9.8 %shard_map.140 = f32[16,16,128]{2,1,0:T(8,128)} custom-call(f32[16,128]{1,0:T(8,128)} %pad_bitcast_fusion.x_ref), custom_call_target="tpu_custom_call" | custom-call | tf_op jit(solution)/shard_map/pallas_call | solution.py:74
  325.4 10.4 %collective-permute-done.30 = bf16[1,32,7168]{2,1,0:T(8,128)(2,1)S(1)} collective-permute-done((bf16[1,32,7168]{2,1,0:T(8,128)(2,1)S(1)}, bf16[1,32,7168]{2,1,0:T(8,128)(2,1)S(1)}, u32[]{:S(2)}, u32[]{:S(2)}) %collective-permute-start.30) | collective-permute-done | bytes 458784 | tf_op jit(solution)/shard_map/ppermute | solution.py:101
  (251 shorter events, 82.6 us)
Async XLA Ops:
  2.2 30.2 %collective-permute-start = (bf16[1,32,7168]{2,1,0:T(8,128)(2,1)S(1)}, bf16[1,32,7168]{2,1,0:T(8,128)(2,1)S(1)}, u32[]{:S(2)}, u32[]{:S(2)}) collective-permute-start(bf16[1,32,7168]{2,1,0:T(8,128)(2,1)S(1)} %get-tuple-element.43), channel_id=1, source_target_pairs={{0,4},{4,0},{1,5},{5,1},{2,6},{6,2},{3,7},{7,3},{8,12},{12,8},{9,1... | collective-permute-start | bytes 1376264 | tf_op jit(solution)/shard_map/ppermute | solution.py:101
  5.2 25.1 %collective-permute-start.5 = (bf16[1,32,7168]{2,1,0:T(8,128)(2,1)S(1)}, bf16[1,32,7168]{2,1,0:T(8,128)(2,1)S(1)}, u32[]{:S(2)}, u32[]{:S(2)}) collective-permute-start(bf16[1,32,7168]{2,1,0:T(8,128)(2,1)S(1)} %get-tuple-element.42), channel_id=1, source_target_pairs={{0,16},{8,24},{16,0},{24,8},{1,17},{9,25},{17,1},{25,9},{2,18},{10... | collective-permute-start | bytes 1376264 | tf_op jit(solution)/shard_map/ppermute | solution.py:101
  6.8 60.9 %collective-permute-start.10 = (bf16[1,32,7168]{2,1,0:T(8,128)(2,1)S(1)}, bf16[1,32,7168]{2,1,0:T(8,128)(2,1)}, u32[]{:S(2)}, u32[]{:S(2)}) collective-permute-start(bf16[1,32,7168]{2,1,0:T(8,128)(2,1)S(1)} %get-tuple-element.40), channel_id=1, source_target_pairs={{0,4},{4,0},{1,5},{5,1},{2,6},{6,2},{3,7},{7,3},{8,12},{12,8},{9,1... | collective-permute-start | bytes 1376264 | tf_op jit(solution)/shard_map/ppermute | solution.py:101
  7.3 62.2 %collective-permute-start.12 = (bf16[1,32,7168]{2,1,0:T(8,128)(2,1)S(1)}, bf16[1,32,7168]{2,1,0:T(8,128)(2,1)S(1)}, u32[]{:S(2)}, u32[]{:S(2)}) collective-permute-start(bf16[1,32,7168]{2,1,0:T(8,128)(2,1)S(1)} %get-tuple-element.41), channel_id=1, source_target_pairs={{0,16},{8,24},{16,0},{24,8},{1,17},{9,25},{17,1},{25,9},{2,18},{10... | collective-permute-start | bytes 1376264 | tf_op jit(solution)/shard_map/ppermute | solution.py:101
  30.4 21.3 %collective-permute-start.6 = (bf16[2,32,7168]{2,1,0:T(8,128)(2,1)S(1)}, bf16[2,32,7168]{2,1,0:T(8,128)(2,1)S(1)}, u32[]{:S(2)}, u32[]{:S(2)}) collective-permute-start(bf16[2,32,7168]{2,1,0:T(8,128)(2,1)S(1)} %pad_maximum_fusion.5), channel_id=1, source_target_pairs={{0,4},{4,0},{1,5},{5,1},{2,6},{6,2},{3,7},{7,3},{8,12},{12,8},{9,1... | collective-permute-start | bytes 2752520 | tf_op jit(solution)/shard_map/ppermute | solution.py:101
  32.5 20.8 %collective-permute-start.1 = (bf16[2,32,7168]{2,1,0:T(8,128)(2,1)S(1)}, bf16[2,32,7168]{2,1,0:T(8,128)(2,1)S(1)}, u32[]{:S(2)}, u32[]{:S(2)}) collective-permute-start(bf16[2,32,7168]{2,1,0:T(8,128)(2,1)S(1)} %pad_maximum_fusion.4), channel_id=1, source_target_pairs={{0,16},{8,24},{16,0},{24,8},{1,17},{9,25},{17,1},{25,9},{2,18},{10... | collective-permute-start | bytes 2752520 | tf_op jit(solution)/shard_map/ppermute | solution.py:101
  53.8 18.8 %collective-permute-start.7 = (bf16[2,4,32,7168]{3,2,1,0:T(8,128)(2,1)S(1)}, bf16[2,4,32,7168]{3,2,1,0:T(8,128)(2,1)}, u32[]{:S(2)}, u32[]{:S(2)}) collective-permute-start(bf16[2,4,32,7168]{3,2,1,0:T(8,128)(2,1)S(1)} %pad_maximum_fusion), channel_id=1, source_target_pairs={{0,8},{8,0},{16,24},{24,16},{1,9},{9,1},{17,25},{25,17},{2,10},{10... | collective-permute-start | bytes 11010056 | tf_op jit(solution)/shard_map/ppermute | solution.py:101
  56.0 15.2 %collective-permute-start.3 = (bf16[2,2,2,8,1024]{4,3,2,1,0:T(8,128)(2,1)S(1)}, bf16[2,2,2,8,1024]{4,3,2,1,0:T(8,128)(2,1)S(1)}, u32[]{:S(2)}, u32[]{:S(2)}) collective-permute-start(bf16[2,2,2,8,1024]{4,3,2,1,0:T(8,128)(2,1)S(1)} %get-tuple-element.66), channel_id=1, source_target_pairs={{0,16},{8,24},{16,0},{24,8},{1,17},{9,25},{17,1},{25,9},{2,18},{10... | collective-permute-start | bytes 393224 | tf_op jit(solution)/shard_map/ppermute | solution.py:101
  57.6 14.2 %collective-permute-start.4 = (bf16[2,2,2,8,1024]{4,3,2,1,0:T(8,128)(2,1)S(1)}, bf16[2,2,2,8,1024]{4,3,2,1,0:T(8,128)(2,1)S(1)}, u32[]{:S(2)}, u32[]{:S(2)}) collective-permute-start(bf16[2,2,2,8,1024]{4,3,2,1,0:T(8,128)(2,1)S(1)} %get-tuple-element.65), channel_id=1, source_target_pairs={{0,24},{8,16},{16,8},{24,0},{1,25},{9,17},{17,9},{25,1},{2,26},{10... | collective-permute-start | bytes 393224 | tf_op jit(solution)/shard_map/ppermute | solution.py:101
  69.5 22.3 %collective-permute-start.11 = (bf16[2,32,7168]{2,1,0:T(8,128)(2,1)S(1)}, bf16[2,32,7168]{2,1,0:T(8,128)(2,1)S(1)}, u32[]{:S(2)}, u32[]{:S(2)}) collective-permute-start(bf16[2,32,7168]{2,1,0:T(8,128)(2,1)S(1)} %fusion.49), channel_id=1, source_target_pairs={{0,16},{8,24},{16,0},{24,8},{1,17},{9,25},{17,1},{25,9},{2,18},{10... | collective-permute-start | bytes 2752520 | tf_op jit(solution)/shard_map/ppermute | solution.py:101
  71.3 24.3 %collective-permute-start.13 = (bf16[2,32,7168]{2,1,0:T(8,128)(2,1)S(1)}, bf16[2,32,7168]{2,1,0:T(8,128)(2,1)S(1)}, u32[]{:S(2)}, u32[]{:S(2)}) collective-permute-start(bf16[2,32,7168]{2,1,0:T(8,128)(2,1)S(1)} %fusion.52), channel_id=1, source_target_pairs={{0,4},{4,0},{1,5},{5,1},{2,6},{6,2},{3,7},{7,3},{8,12},{12,8},{9,1... | collective-permute-start | bytes 2752520 | tf_op jit(solution)/shard_map/ppermute | solution.py:101
  110.5 37.5 %collective-permute-start.14 = (bf16[2,4,32,7168]{3,2,1,0:T(8,128)(2,1)}, bf16[2,4,32,7168]{3,2,1,0:T(8,128)(2,1)}, u32[]{:S(2)}, u32[]{:S(2)}) collective-permute-start(bf16[2,4,32,7168]{3,2,1,0:T(8,128)(2,1)} %maximum_add_fusion), channel_id=1, source_target_pairs={{0,8},{8,0},{16,24},{24,16},{1,9},{9,1},{17,25},{25,17},{2,10},{10... | collective-permute-start | bytes 11010056 | tf_op jit(solution)/shard_map/ppermute | solution.py:101
  119.7 14.9 %collective-permute-start.17 = (bf16[16,1,8,1024]{3,2,0,1:T(8,128)(2,1)S(1)}, bf16[16,1,8,1024]{3,2,0,1:T(8,128)(2,1)S(1)}, u32[]{:S(2)}, u32[]{:S(2)}) collective-permute-start(bf16[16,1,8,1024]{3,2,0,1:T(8,128)(2,1)S(1)} %get-tuple-element.55), channel_id=1, source_target_pairs={{0,2},{1,3},{2,0},{3,1},{4,6},{5,7},{6,4},{7,5},{8,10},{9,11},{10,... | collective-permute-start | bytes 786440 | tf_op jit(solution)/shard_map/ppermute | solution.py:101
  164.2 40.3 %collective-permute-start.21 = (bf16[2,4,32,7168]{3,2,1,0:T(8,128)(2,1)}, bf16[2,4,32,7168]{3,2,1,0:T(8,128)(2,1)}, u32[]{:S(2)}, u32[]{:S(2)}) collective-permute-start(bf16[2,4,32,7168]{3,2,1,0:T(8,128)(2,1)} %fusion.24), channel_id=1, source_target_pairs={{0,8},{8,0},{16,24},{24,16},{1,9},{9,1},{17,25},{25,17},{2,10},{10... | collective-permute-start | bytes 11010056 | tf_op jit(solution)/shard_map/ppermute | solution.py:101
  164.8 14.4 %collective-permute-start.15 = (bf16[16,2,8,1024]{3,2,0,1:T(8,128)(2,1)S(1)}, bf16[16,2,8,1024]{3,2,0,1:T(8,128)(2,1)S(1)}, u32[]{:S(2)}, u32[]{:S(2)}) collective-permute-start(bf16[16,2,8,1024]{3,2,0,1:T(8,128)(2,1)S(1)} %fusion.54), channel_id=1, source_target_pairs={{0,1},{1,0},{2,3},{3,2},{4,5},{5,4},{6,7},{7,6},{8,9},{9,8},{10,11... | collective-permute-start | bytes 1572872 | tf_op jit(solution)/shard_map/ppermute | solution.py:101
  180.2 14.4 %collective-permute-start.16 = (bf16[16,1,8,1024]{3,2,0,1:T(8,128)(2,1)}, bf16[16,1,8,1024]{3,2,0,1:T(8,128)(2,1)S(1)}, u32[]{:S(2)}, u32[]{:S(2)}) collective-permute-start(bf16[16,1,8,1024]{3,2,0,1:T(8,128)(2,1)} %fusion.70), channel_id=1, source_target_pairs={{0,2},{1,3},{2,0},{3,1},{4,6},{5,7},{6,4},{7,5},{8,10},{9,11},{10,... | collective-permute-start | bytes 786440 | tf_op jit(solution)/shard_map/ppermute | solution.py:101
  204.5 14.4 %collective-permute-start.19 = (bf16[16,1,8,1024]{3,2,0,1:T(8,128)(2,1)}, bf16[16,1,8,1024]{3,2,0,1:T(8,128)(2,1)}, u32[]{:S(2)}, u32[]{:S(2)}) collective-permute-start(bf16[16,1,8,1024]{3,2,0,1:T(8,128)(2,1)} %get-tuple-element.52), channel_id=1, source_target_pairs={{0,2},{1,3},{2,0},{3,1},{4,6},{5,7},{6,4},{7,5},{8,10},{9,11},{10,... | collective-permute-start | bytes 786440 | tf_op jit(solution)/shard_map/ppermute | solution.py:101
  215.0 22.4 %collective-permute-start.22 = (bf16[2,32,7168]{2,1,0:T(8,128)(2,1)S(1)}, bf16[2,32,7168]{2,1,0:T(8,128)(2,1)S(1)}, u32[]{:S(2)}, u32[]{:S(2)}) collective-permute-start(bf16[2,32,7168]{2,1,0:T(8,128)(2,1)S(1)} %get-tuple-element.33), channel_id=1, source_target_pairs={{0,4},{4,0},{1,5},{5,1},{2,6},{6,2},{3,7},{7,3},{8,12},{12,8},{9,1... | collective-permute-start | bytes 2752520 | tf_op jit(solution)/shard_map/ppermute | solution.py:101
  216.4 22.1 %collective-permute-start.24 = (bf16[2,32,7168]{2,1,0:T(8,128)(2,1)S(1)}, bf16[2,32,7168]{2,1,0:T(8,128)(2,1)S(1)}, u32[]{:S(2)}, u32[]{:S(2)}) collective-permute-start(bf16[2,32,7168]{2,1,0:T(8,128)(2,1)S(1)} %get-tuple-element.32), channel_id=1, source_target_pairs={{0,16},{8,24},{16,0},{24,8},{1,17},{9,25},{17,1},{25,9},{2,18},{10... | collective-permute-start | bytes 2752520 | tf_op jit(solution)/shard_map/ppermute | solution.py:101
  241.0 17.7 %collective-permute-start.25 = (bf16[1,32,7168]{2,1,0:T(8,128)(2,1)}, bf16[1,32,7168]{2,1,0:T(8,128)(2,1)}, u32[]{:S(2)}, u32[]{:S(2)}) collective-permute-start(bf16[1,32,7168]{2,1,0:T(8,128)(2,1)} %slice.504), channel_id=1, source_target_pairs={{0,4},{4,0},{1,5},{5,1},{2,6},{6,2},{3,7},{7,3},{8,12},{12,8},{9,1... | collective-permute-start | bytes 1376264 | tf_op jit(solution)/shard_map/ppermute | solution.py:101
  250.1 16.2 %collective-permute-start.23 = (bf16[2,4,32,7168]{3,2,1,0:T(8,128)(2,1)}, bf16[2,4,32,7168]{3,2,1,0:T(8,128)(2,1)}, u32[]{:S(2)}, u32[]{:S(2)}) collective-permute-start(bf16[2,4,32,7168]{3,2,1,0:T(8,128)(2,1)} %fusion.27), channel_id=1, source_target_pairs={{0,8},{8,0},{16,24},{24,16},{1,9},{9,1},{17,25},{25,17},{2,10},{10... | collective-permute-start | bytes 11010056 | tf_op jit(solution)/shard_map/ppermute | solution.py:101
  277.6 26.6 %collective-permute-start.27 = (bf16[2,32,7168]{2,1,0:T(8,128)(2,1)}, bf16[2,32,7168]{2,1,0:T(8,128)(2,1)S(1)}, u32[]{:S(2)}, u32[]{:S(2)}) collective-permute-start(bf16[2,32,7168]{2,1,0:T(8,128)(2,1)} %get-tuple-element.34), channel_id=1, source_target_pairs={{0,16},{8,24},{16,0},{24,8},{1,17},{9,25},{17,1},{25,9},{2,18},{10... | collective-permute-start | bytes 2752520 | tf_op jit(solution)/shard_map/ppermute | solution.py:101
  279.0 26.1 %collective-permute-start.29 = (bf16[2,32,7168]{2,1,0:T(8,128)(2,1)S(1)}, bf16[2,32,7168]{2,1,0:T(8,128)(2,1)}, u32[]{:S(2)}, u32[]{:S(2)}) collective-permute-start(bf16[2,32,7168]{2,1,0:T(8,128)(2,1)S(1)} %get-tuple-element.35), channel_id=1, source_target_pairs={{0,4},{4,0},{1,5},{5,1},{2,6},{6,2},{3,7},{7,3},{8,12},{12,8},{9,1... | collective-permute-start | bytes 2752520 | tf_op jit(solution)/shard_map/ppermute | solution.py:101
  309.3 14.8 %collective-permute-start.28 = (bf16[1,32,7168]{2,1,0:T(8,128)(2,1)S(1)}, bf16[1,32,7168]{2,1,0:T(8,128)(2,1)}, u32[]{:S(2)}, u32[]{:S(2)}) collective-permute-start(bf16[1,32,7168]{2,1,0:T(8,128)(2,1)S(1)} %slice.502), channel_id=1, source_target_pairs={{0,4},{4,0},{1,5},{5,1},{2,6},{6,2},{3,7},{7,3},{8,12},{12,8},{9,1... | collective-permute-start | bytes 1376264 | tf_op jit(solution)/shard_map/ppermute | solution.py:101
  (35 other events, 454.4 us)
